TPU v7x, 128 devices: a whole 4x4x4 slice. The times are simulated.
128 devices in a mesh: grp: 4 (over x), wide: 32 (over y, z, core).
Axes of the slice: x: 4, y: 4, z: 4, core: 2. Of those that a mesh axis runs over, the one named last changes fastest.
Arguments:
- fine_pop: float32 [256, 19, 4096], P(('grp', 'wide')), may hold values from 0 to 1, as said below
- coarse_pop: float32 [19, 32, 8, 4096], P(None, 'grp', None, 'wide'), may hold values from 0 to 1, as said below
- new_slot: int32 [256], replicated, may hold values from 0 to 255, each once
Outputs:
- fine_out: float32 [256, 19, 4096], P(('grp', 'wide'))
- coarse_out: float32 [19, 32, 8, 4096], P(None, 'grp', None, 'wide')
Inputs may be any that keep to these rules, and one draw needn't show every extreme that they name: A permutation: fine block b moves to slot new_slot[b]. `fine_pop`: positive populations near equilibrium, densities of order one, speeds under 0.25. `coarse_pop`: positive populations near equilibrium, densities of order one, speeds under 0.25.
All inputs are finite; a program needn't handle non-finite values.
Results may differ from a plain program's by a relative error of at most 0.00002.
Values sent between devices are 32-bit elements; how exact they have to be, the bound alone decides.
A program may use at most 128 MiB of HBM per device.

v0:
```python
import jax
import jax.numpy as jnp
from jax import lax
from jax.experimental import pallas as pl
from jax.experimental.pallas import tpu as pltpu
from jax.sharding import PartitionSpec as P

VELOCITIES = (
    (0, 0, 0),
    (1, 0, 0),
    (-1, 0, 0),
    (0, 1, 0),
    (0, -1, 0),
    (0, 0, 1),
    (0, 0, -1),
    (1, 1, 0),
    (-1, -1, 0),
    (1, -1, 0),
    (-1, 1, 0),
    (1, 0, 1),
    (-1, 0, -1),
    (1, 0, -1),
    (-1, 0, 1),
    (0, 1, 1),
    (0, -1, -1),
    (0, 1, -1),
    (0, -1, 1),
)
WEIGHTS = (1.0 / 3.0,) + (1.0 / 18.0,) * 6 + (1.0 / 36.0,) * 12
COUPLING = -5.0
FINE_TAU = 1.1
COARSE_TAU = 0.8
TO_COARSE = 2.0 * COARSE_TAU / FINE_TAU
TO_FINE = FINE_TAU / (2.0 * COARSE_TAU)

INDEX = {c: i for i, c in enumerate(VELOCITIES)}
X_PLUS = (1, 7, 9, 11, 13)
X_MINUS = tuple(INDEX[(-c[0], c[1], c[2])] for c in (VELOCITIES[i] for i in X_PLUS))
Y_PLUS = (3, 7, 10, 15, 17)
Y_MINUS = tuple(INDEX[(c[0], -c[1], c[2])] for c in (VELOCITIES[i] for i in Y_PLUS))

OFFSETS = sorted(
    ((a, b, c, d) for a in range(4) for b in range(4) for c in range(4) for d in range(2) if a + b + c + d),
    key=lambda o: (-sum(min(v, 4 - v) for v in o[:3]), (o[0] * 7 + o[1] * 5 + o[2] * 3 + o[3]) % 11),
)


def send(src, dst, sems, device):
    return pltpu.make_async_remote_copy(
        src_ref=src,
        dst_ref=dst,
        send_sem=sems.at[0],
        recv_sem=sems.at[1],
        device_id=device,
        device_id_type=pl.DeviceIdType.MESH,
    )


def device_of(offset):
    g, w = lax.axis_index("grp"), lax.axis_index("wide")
    x = lax.rem(g + offset[0], 4)
    y = lax.rem(w // 8 + offset[1], 4)
    z = lax.rem(lax.rem(w // 2, 4) + offset[2], 4)
    c = lax.rem(lax.rem(w, 2) + offset[3], 2)
    return x, (y * 4 + z) * 2 + c


def lane():
    return lax.broadcasted_iota(jnp.int32, (8, 128), 1)


def sub():
    return lax.broadcasted_iota(jnp.int32, (8, 128), 0)


def rot(v, shift):
    return pltpu.roll(v, shift % 128, 1)


def turn(v, shift):
    return pltpu.roll(v, shift % 8, 0)


def potential(density):
    return 1.0 - jnp.exp(-density)


def moments(state):
    density = state[0]
    momentum = [None, None, None]
    for d in range(1, 19):
        density = density + state[d]
        for a in range(3):
            c = VELOCITIES[d][a]
            if c:
                m = momentum[a]
                momentum[a] = c * state[d] if m is None else (m + state[d] if c > 0 else m - state[d])
    return [density] + momentum


def relax(density, velocity, states, keep, gain):
    base = 1.0 - 1.5 * (velocity[0] * velocity[0] + velocity[1] * velocity[1] + velocity[2] * velocity[2])
    scaled = {w: (gain * w) * density for w in set(WEIGHTS[d] for d, _ in states)}
    entries = []
    for d, h in states:
        along = None
        for a in range(3):
            c = VELOCITIES[d][a]
            if c:
                term = velocity[a] if c > 0 else -velocity[a]
                along = term if along is None else along + term
        shape = base if along is None else base + along * (3.0 + 4.5 * along)
        entries.append(keep * h + scaled[WEIGHTS[d]] * shape)
    return entries


def collide(mom, pot, grad, states, tau, flip=None):
    inverse = 1.0 / mom[0]
    push = (-tau * COUPLING) * pot
    velocity = [(mom[1 + a] + push * grad[a]) * inverse for a in range(3)]
    if flip is not None:
        velocity[0] = velocity[0] * flip
    return relax(mom[0], velocity, states, 1.0 - 1.0 / tau, 1.0 / tau)


def fine_y(tiles, step, ghost):
    e = lane() & 15
    out = [None] * 8
    edge, inner, outer = (15, 0, 1) if step > 0 else (0, 1, 0)
    for r in range(4):
        across = rot(tiles[outer * 4 + r], 15 * step)
        out[inner * 4 + r] = jnp.where(e == edge, across, rot(tiles[inner * 4 + r], -step))
        out[outer * 4 + r] = jnp.where(e == edge, ghost[r], rot(tiles[outer * 4 + r], -step))
    return out


def fine_z(tiles, step):
    c = lane() >> 4
    moved = [rot(t, -16 * step) for t in tiles]
    edge = 7 if step > 0 else 0
    return [jnp.where(c == edge, moved[j ^ 1], moved[j]) for j in range(len(tiles))]


def fine_x(tiles, step, rows):
    s = sub()
    out = [None] * 8
    for k in range(2):
        for h in range(2):
            low, high = k * 4 + h, k * 4 + 2 + h
            if step > 0:
                out[low] = tiles[high]
                out[high] = jnp.where(s == 7, rows(4 + k * 2 + h), turn(tiles[low], -1))
            else:
                out[high] = tiles[low]
                out[low] = jnp.where(s == 0, rows(k * 2 + h), turn(tiles[high], 1))
    return out


def side_y(tile, step, ghost):
    e, k = lane() & 15, (sub() >> 1) & 1
    edge, inner = (15, 0) if step > 0 else (0, 1)
    across = turn(rot(tile, 15 * step), -2 * step)
    return jnp.where(e == edge, jnp.where(k == inner, across, ghost), rot(tile, -step))


def side_z(tile, step):
    c, h = lane() >> 4, sub() & 1
    moved = rot(tile, -16 * step)
    other = jnp.where(h == 0, turn(moved, -1), turn(moved, 1))
    return jnp.where(c == (7 if step > 0 else 0), other, moved)


def stencil(pot, up, down, back, front):
    total = pot * (1.0 / 18.0) + (up + down + back + front) * (1.0 / 36.0)
    return total, up - down, back - front


def rowcast(row):
    return jnp.broadcast_to(row, (8, 128))


def fine_step(state, mom, ghost_pot, ghost_post, ghost_side, halo, put, work):
    post, tee, face, rows = work
    pots = [mom[4, j] for j in range(8)]
    gp = [ghost_pot[h] for h in range(2)] * 2
    gz = fine_z(gp, 1)
    gz = [a - b for a, b in zip(gz, fine_z(gp, -1))]
    up, down = fine_y(pots, 1, gp), fine_y(pots, -1, gp)
    back, front = fine_z(pots, 1), fine_z(pots, -1)
    parts = [stencil(*v) for v in zip(pots, up, down, back, front)]
    total, dy, dz = ([p[i] for p in parts] for i in range(3))
    zz = [a + b for a, b in zip(fine_z(dy, 1), fine_z(dy, -1))]
    yy = [a + b for a, b in zip(fine_y(dz, 1, gz), fine_y(dz, -1, gz))]
    for j in range(8):
        tee[0, j] = total[j]
        tee[1, j] = dy[j] * (1.0 / 18.0) + zz[j] * (1.0 / 36.0)
        tee[2, j] = dz[j] * (1.0 / 18.0) + yy[j] * (1.0 / 36.0)
        tee[3, j] = dy[j]
        tee[4, j] = dz[j]

    def finish():
        flip = jnp.where(sub() < 4, 1.0, -1.0)
        near, far, own = potential(halo[0]), halo[9], face[...]
        outer, inner = ghost_side[0], ghost_side[1]

        def terms(tile, ghost):
            return stencil(tile, side_y(tile, 1, ghost), side_y(tile, -1, ghost), side_z(tile, 1), side_z(tile, -1))

        t1, y1, z1 = terms(near, outer)
        t2, y2, z2 = terms(far, outer)
        t0, y0, z0 = terms(own, inner)
        goz = side_z(outer, 1) - side_z(outer, -1)
        grad = [
            (t0 - t2) * flip,
            y1 * (1.0 / 18.0) + (y0 + y2 + side_z(y1, 1) + side_z(y1, -1)) * (1.0 / 36.0),
            z1 * (1.0 / 18.0) + (z0 + z2 + side_y(z1, 1, goz) + side_y(z1, -1, goz)) * (1.0 / 36.0),
        ]
        states = [(d, halo[4 + q]) for q, d in enumerate(X_PLUS)]
        for q, v in enumerate(collide([halo[i] for i in range(4)], near, grad, states, FINE_TAU, flip)):
            rows[q] = v
        rows[5], rows[6], rows[7] = t1, y1, z1

        def row(i):
            return lambda r: rowcast(rows[i, r : r + 1, :])

        total, dy, dz = ([tee[i, j] for j in range(8)] for i in (0, 3, 4))
        gx = [a - b for a, b in zip(fine_x(total, 1, row(5)), fine_x(total, -1, row(5)))]
        xy = [a + b for a, b in zip(fine_x(dy, 1, row(6)), fine_x(dy, -1, row(6)))]
        xz = [a + b for a, b in zip(fine_x(dz, 1, row(7)), fine_x(dz, -1, row(7)))]
        for j in range(8):
            tee[0, j] = gx[j]
            tee[1, j] = tee[1, j] + xy[j] * (1.0 / 36.0)
            tee[2, j] = tee[2, j] + xz[j] * (1.0 / 36.0)

        def body(j, _):
            values = collide(
                [mom[i, j] for i in range(4)],
                mom[4, j],
                [tee[i, j] for i in range(3)],
                [(d, state[d, j]) for d in range(19)],
                FINE_TAU,
            )
            for d in range(19):
                post[d, j] = values[d]
            return 0

        lax.fori_loop(0, 8, body, 0)
        for d in range(19):
            tiles = [post[d, j] for j in range(8)]
            cx, cy, cz = VELOCITIES[d]
            if cx:
                tiles = fine_x(tiles, -cx, row((X_PLUS if cx > 0 else X_MINUS).index(d)))
            if cz:
                tiles = fine_z(tiles, -cz)
            if cy:
                q = (Y_PLUS if cy > 0 else Y_MINUS).index(d)
                tiles = fine_y(tiles, -cy, [ghost_post[q, r] for r in range(4)])
            put(d, tiles)

    return finish


def fine_moments(state, mom):
    def body(j, _):
        values = moments([state[d, j] for d in range(19)])
        for i in range(4):
            mom[i, j] = values[i]
        mom[4, j] = potential(values[0])
        return 0

    lax.fori_loop(0, 8, body, 0)


def fine_faces(state, mom, out, face):
    for k in range(2):
        for h in range(2):
            r, low, high = k * 2 + h, k * 4 + h, k * 4 + 2 + h
            for i in range(4):
                out[i, r : r + 1, :] = mom[i, high, 7:8, :]
                out[i, 4 + r : 5 + r, :] = mom[i, low, 0:1, :]
            for q in range(5):
                out[4 + q, r : r + 1, :] = state[X_PLUS[q], high, 7:8, :]
                out[4 + q, 4 + r : 5 + r, :] = state[X_MINUS[q], low, 0:1, :]
            out[9, r : r + 1, :] = mom[4, low, 7:8, :]
            out[9, 4 + r : 5 + r, :] = mom[4, high, 0:1, :]
            face[r : r + 1, :] = mom[4, low, 0:1, :]
            face[4 + r : 5 + r, :] = mom[4, high, 7:8, :]


def kernel(
    fine, coarse, slots, fine_out, coarse_out,
    p1, r1, p2, r2, inv_v, inv_s,
    state, post, mom, tee, face, rows, out1, out2, halo1, halo2,
    layers, low_out, low_in, ghost, edge_r, edge_l, edge_in, ghost_post, ghost_side,
    cmom, face_c, halo_c, rest, rest_out, rest_in, ghost_t, ghost_c, ctee, cpost,
    s1, s2, s3, sg, se, sc, sm, sh1, sh2, sr, sx,
):
    g, w = lax.axis_index("grp"), lax.axis_index("wide")
    me = g * 32 + w
    right, left = lax.rem(g + 1, 4), lax.rem(g + 3, 4)
    ahead, behind = lax.rem(w + 1, 32), lax.rem(w + 31, 32)
    barrier = pltpu.get_barrier_semaphore()
    for offset in OFFSETS:
        pl.semaphore_signal(barrier, inc=1, device_id=device_of(offset), device_id_type=pl.DeviceIdType.MESH)

    def pack(t, _):
        for k in range(2):
            v = fine[k, :, pl.ds(pl.multiple_of(t * 128, 128), 128)]
            for q in range(4):
                n = min(5, 19 - 5 * q)
                p1[k, t * 4 + q, 0:n, :] = v[5 * q : 5 * q + n]
        return 0

    lax.fori_loop(0, 32, pack, 0)

    place = sub() * 128 + lane()

    def invert(b, acc):
        return jnp.where(place == slots[b], b, acc)

    inv_v[...] = lax.fori_loop(0, 256, invert, jnp.zeros((8, 128), jnp.int32), unroll=8)
    fetch = pltpu.make_async_copy(inv_v, inv_s, s3)
    fetch.start()
    for k in range(2):
        r1[2 * me + k, 0:5, :] = p1[k, me, 0:5, :]

    def coarse_body(i, _):
        values = moments([coarse[d, i] for d in range(19)])
        for a in range(4):
            cmom[a, i + 2] = values[a]
        cmom[4, i + 2] = potential(values[0])
        return 0

    lax.fori_loop(0, 8, coarse_body, 0)
    for q in range(5):
        face_c[0, q] = coarse[X_PLUS[q], 7]
        face_c[1, q] = coarse[X_MINUS[q], 0]

    flat = coarse.reshape(19 * 64, 128)
    e, c_l, s = lane() & 15, lane() >> 4, sub()

    def layer_body(d, _):
        for h in range(2):
            v = None
            for m in range(4):
                t = rot(flat[pl.ds(d * 64 + h * 4 + m, 8, stride=8), :], 32 * m + 15)
                v = t if v is None else jnp.where(c_l >= 2 * m, t, v)
            layers[d, h] = v
        return 0

    lax.fori_loop(0, 19, layer_body, 0)

    def rescaled(source, is_low, factor, h):
        m = moments([source[d, h] for d in range(19)])
        inverse = 1.0 / m[0]
        u = [m[1] * inverse, m[2] * inverse * jnp.where(is_low, 1.0, -1.0), m[3] * inverse]
        states = [(d, jnp.where(is_low, source[d, h], source[Y_MINUS[q], h])) for q, d in enumerate(Y_PLUS)]
        return relax(m[0], u, states, factor, 1.0 - factor) + [potential(m[0])]

    for h in range(2):
        for q, v in enumerate(rescaled(layers, e == 14, TO_FINE, h)):
            low_out[q, h] = jnp.where((c_l & 1) == 1, rot(v, 16), v)

    pl.semaphore_wait(barrier, len(OFFSETS))
    to_ahead = send(low_out, low_in, sg, (g, ahead))
    to_ahead.start()
    for offset in OFFSETS:
        x, y = device_of(offset)
        send(p1.at[:, x * 32 + y, 0:5, :], r1.at[pl.ds(2 * me, 2), 0:5, :], s1, (x, y)).start()
    cm_r = send(cmom.at[:, 8:10], cmom.at[:, 0:2], sm.at[0], (right, w))
    cm_l = send(cmom.at[:, 2:4], cmom.at[:, 10:12], sm.at[1], (left, w))
    cf_r = send(face_c.at[0], halo_c.at[0], sc.at[0], (right, w))
    cf_l = send(face_c.at[1], halo_c.at[1], sc.at[1], (left, w))
    for copy in (cm_r, cm_l, cf_r, cf_l):
        copy.start()

    to_ahead.wait()
    for q in range(6):
        for h in range(2):
            v = jnp.where(e == 0, rot(low_in[q, h], -14), low_out[q, h])
            ghost[q, h] = v
            edge_r[q * 2 + h : q * 2 + h + 1, :] = v[7:8]
            edge_l[q * 2 + h : q * 2 + h + 1, :] = v[0:1]
    ge_r = send(edge_r, edge_in.at[0], se.at[0], (right, w))
    ge_l = send(edge_l, edge_in.at[1], se.at[1], (left, w))
    ge_r.start()
    ge_l.start()

    fetch.wait()
    all1 = r1.at[0:254, 0:5, :]
    pltpu.make_async_copy(all1, all1, s1.at[1]).wait()

    def permute(m, _):
        for k in range(2):
            slot = 2 * m + k
            p2[k, m, 0:5, :] = r1[inv_s[slot // 128, lax.rem(slot, 128)], 0:5, :]
        return 0

    lax.fori_loop(0, 128, permute, 0, unroll=4)
    for k in range(2):
        r2[k, me, 0:5, :] = p2[k, me, 0:5, :]
    for offset in OFFSETS:
        x, y = device_of(offset)
        send(p2.at[:, x * 32 + y, 0:5, :], r2.at[:, me, 0:5, :], s2, (x, y)).start()

    ge_r.wait()
    ge_l.wait()
    for q in range(5):
        v = [ghost[q, h] for h in range(2)]
        cx, _, cz = VELOCITIES[Y_PLUS[q]]
        if cz:
            v = fine_z(v, -cz)
        for h in range(2):
            low = high = v[h]
            if cx > 0:
                low = jnp.where(s == 0, rowcast(edge_in[0, q * 2 + h : q * 2 + h + 1, :]), turn(v[h], 1))
            if cx < 0:
                high = jnp.where(s == 7, rowcast(edge_in[1, q * 2 + h : q * 2 + h + 1, :]), turn(v[h], -1))
            ghost_post[q, h] = low
            ghost_post[q, 2 + h] = high
    for k in range(2):
        for h in range(2):
            r = k * 2 + h
            ghost_side[0, r : r + 1, :] = edge_in[0, 10 + h : 11 + h, :]
            ghost_side[0, 4 + r : 5 + r, :] = edge_in[1, 10 + h : 11 + h, :]
            ghost_side[1, r : r + 1, :] = ghost[5, h, 0:1, :]
            ghost_side[1, 4 + r : 5 + r, :] = ghost[5, h, 7:8, :]
    for copy in (cm_r, cm_l, cf_r, cf_l):
        copy.wait()

    all2 = r2.at[:, 0:127, 0:5, :]
    pltpu.make_async_copy(all2, all2, s2.at[1]).wait()
    got = r2.reshape(2048, 128)
    for d in range(19):
        for k in range(2):
            for r in range(4):
                state[d, k * 4 + r] = got[pl.ds(((k * 128 + r * 4 + d // 5) * 8) + d % 5, 8, stride=128), :]

    fine_moments(state, mom)
    fine_faces(state, mom, out1, face)
    f1r = send(out1.at[:, 0:4], halo1.at[:, 0:4], sh1.at[0], (right, w))
    f1l = send(out1.at[:, 4:8], halo1.at[:, 4:8], sh1.at[1], (left, w))
    f1r.start()
    f1l.start()

    for d in range(19):
        for h in range(2):
            v = jnp.where(e < 8, state[d, h] + state[d, 2 + h], state[d, 4 + h] + state[d, 6 + h])
            v = v + rot(v, -1)
            rest[d, h] = 0.125 * (v + rot(v, -16))
    for h in range(2):
        for q, v in enumerate(rescaled(rest, e == 14, TO_COARSE, h)):
            rest_out[q, h] = v
    to_behind = send(rest_out, rest_in, sr, (g, behind))
    to_behind.start()

    work = (post, tee, face, rows)

    def keep(d, tiles):
        for j in range(8):
            state[d, j] = tiles[j]

    def give(d, tiles):
        for k in range(2):
            for r in range(4):
                fine_out[pl.ds(((k * 3 + d // 8) * 32 + r) * 8 + d % 8, 8, stride=32), :] = tiles[k * 4 + r]

    ghost_pot = [ghost[5, h] for h in range(2)]
    finish = fine_step(state, mom, ghost_pot, ghost_post, ghost_side, halo1, keep, work)
    f1r.wait()
    f1l.wait()
    finish()
    fine_moments(state, mom)
    fine_faces(state, mom, out2, face)
    f2r = send(out2.at[:, 0:4], halo2.at[:, 0:4], sh2.at[0], (right, w))
    f2l = send(out2.at[:, 4:8], halo2.at[:, 4:8], sh2.at[1], (left, w))
    f2r.start()
    f2l.start()

    to_behind.wait()
    turned = ghost_t.reshape(6 * 64, 128)
    last = lane() == 127
    for q in range(6):
        for h in range(2):
            for m in range(4):
                low = rot(rest_out[q, h], -(32 * m + 14))
                ghost_t[q, h * 4 + m] = jnp.where(last, rot(rest_in[q, h], 127 - 32 * m), low)
        for x in range(8):
            ghost_c[q, x + 2] = turned[pl.ds(q * 64 + x, 8, stride=8), :]
    gc_r = send(ghost_c.at[:, 8:10], ghost_c.at[:, 0:2], sx.at[0], (right, w))
    gc_l = send(ghost_c.at[:, 2:4], ghost_c.at[:, 10:12], sx.at[1], (left, w))
    gc_r.start()
    gc_l.start()

    finish = fine_step(state, mom, ghost_pot, ghost_post, ghost_side, halo2, give, work)
    f2r.wait()
    f2l.wait()
    finish()

    gc_r.wait()
    gc_l.wait()

    def coarse_y(v, step, edge):
        return jnp.where(lane() == (127 if step > 0 else 0), edge, rot(v, -step))

    def terms_body(i, _):
        v, edge = cmom[4, i], ghost_c[5, i]
        t, dy, dz = stencil(v, coarse_y(v, 1, edge), coarse_y(v, -1, edge), turn(v, -1), turn(v, 1))
        ctee[0, i], ctee[1, i], ctee[2, i] = t, dy, dz
        return 0

    lax.fori_loop(0, 12, terms_body, 0)

    def coarse_grad(i):
        dy, dz, edge = ctee[1, i], ctee[2, i], ghost_c[5, i]
        edge = turn(edge, -1) - turn(edge, 1)
        return [
            ctee[0, i + 1] - ctee[0, i - 1],
            dy * (1.0 / 18.0) + (ctee[1, i + 1] + ctee[1, i - 1] + turn(dy, 1) + turn(dy, -1)) * (1.0 / 36.0),
            dz * (1.0 / 18.0)
            + (ctee[2, i + 1] + ctee[2, i - 1] + coarse_y(dz, 1, edge) + coarse_y(dz, -1, edge)) * (1.0 / 36.0),
        ]

    def coarse_post(i, states):
        values = collide([cmom[a, i] for a in range(4)], cmom[4, i], coarse_grad(i), states, COARSE_TAU)
        for (d, _), v in zip(states, values):
            cpost[d, i - 1] = v

    def post_body(i, _):
        coarse_post(i + 2, [(d, coarse[d, i]) for d in range(19)])
        return 0

    lax.fori_loop(0, 8, post_body, 0)
    coarse_post(1, [(d, halo_c[0, q]) for q, d in enumerate(X_PLUS)])
    coarse_post(10, [(d, halo_c[1, q]) for q, d in enumerate(X_MINUS)])

    def stream_body(i, _):
        for d in range(19):
            cx, cy, cz = VELOCITIES[d]
            v = cpost[d, i + 1 - cx]
            if cz:
                v = turn(v, cz)
            if cy:
                edge = ghost_c[(Y_PLUS if cy > 0 else Y_MINUS).index(d), i + 2 - cx]
                v = coarse_y(v, -cy, turn(edge, cz) if cz else edge)
            coarse_out[d, i] = v
        return 0

    lax.fori_loop(0, 8, stream_body, 0)
    pltpu.make_async_copy(all1, all1, s1.at[0]).wait()
    pltpu.make_async_copy(all2, all2, s2.at[0]).wait()


def local(fine_pop, coarse_pop, new_slot):
    def tiles(*shape):
        return pltpu.VMEM(shape + (8, 128), jnp.float32)

    def sems(*shape):
        return pltpu.SemaphoreType.DMA(shape)

    vmem = pl.BlockSpec(memory_space=pltpu.VMEM)
    fine_out, coarse_out = pl.pallas_call(
        kernel,
        out_shape=(
            jax.ShapeDtypeStruct((1536, 128), jnp.float32),
            jax.ShapeDtypeStruct((19, 8, 8, 128), jnp.float32),
        ),
        in_specs=[vmem, vmem, pl.BlockSpec(memory_space=pltpu.SMEM)],
        out_specs=(vmem, vmem),
        scratch_shapes=[
            tiles(2, 128), tiles(256), tiles(2, 128), tiles(2, 128),
            pltpu.VMEM((8, 128), jnp.int32), pltpu.SMEM((8, 128), jnp.int32),
            tiles(19, 8), tiles(19, 8), tiles(5, 8), tiles(5, 8), tiles(), tiles(8),
            tiles(10), tiles(10), tiles(10), tiles(10),
            tiles(19, 2), tiles(6, 2), tiles(6, 2), tiles(6, 2),
            pltpu.VMEM((12, 128), jnp.float32), pltpu.VMEM((12, 128), jnp.float32),
            pltpu.VMEM((2, 12, 128), jnp.float32), tiles(5, 4), tiles(2),
            tiles(5, 12), tiles(2, 5), tiles(2, 5), tiles(19, 2), tiles(6, 2), tiles(6, 2),
            tiles(6, 8), tiles(6, 12), tiles(3, 12), tiles(19, 10),
            sems(2), sems(2), pltpu.SemaphoreType.DMA, sems(2), sems(2, 2), sems(2, 2), sems(2, 2),
            sems(2, 2), sems(2, 2), sems(2), sems(2, 2),
        ],
        compiler_params=pltpu.CompilerParams(
            collective_id=0, has_side_effects=True, vmem_limit_bytes=48 * 2**20
        ),
    )(fine_pop, coarse_pop, new_slot)
    fine_out = fine_out.reshape(2, 3, 32, 8, 128).transpose(0, 1, 3, 2, 4).reshape(2, 24, 4096)[:, :19]
    return fine_out, coarse_out


def solution(mesh):
    return jax.shard_map(
        local,
        mesh=mesh,
        in_specs=(P(("grp", "wide"), None, None), P(None, "grp", None, "wide"), P()),
        out_specs=(P(("grp", "wide"), None, None), P(None, "grp", None, "wide")),
        check_vma=False,
    )
```

profile of v0, /device:TPU:0, one launch (start us, length us, event | category | flops | bytes accessed | tf_op | source)
XLA Modules:
  0.0 49.3 jit_solution(14663036703299906040)
XLA Ops:
  0.6 0.0 copy-start.1
  0.6 0.0 copy-start
  0.6 1.5 %copy.5.fine = f32[2,19,4096]{2,1,0:T(8,128)S(1)} copy(f32[2,19,4096]{2,0,1:T(2,128)} %param.3) | data formatting | bytes 1245184 | tf_op args[0]
  2.2 0.0 copy-done.1
  2.2 0.0 copy-done
  2.2 44.8 %shard_map.50 = (f32[1536,128]{1,0:T(8,128)S(1)}, f32[19,8,8,128]{3,2,1,0:T(8,128)S(1)}) custom-call(f32[2,19,4096]{2,1,0:T(8,128)S(1)} %copy.5.fine, f32[19,8,8,128]{3,2,1,0:T(8,128)S(1)} %copy-done, s32[256]{0:T(256)S(1)} %copy-done.1), custom_call_target="tpu_custom_call" | custom-call | tf_op jit(solution)/shard_map/pallas_call | solution.py:562
  47.0 0.1 copy.6
  47.2 0.4 reshape.11
  47.6 0.9 %slice.4 = f32[2,19,4096]{2,0,1:T(2,128)} slice(f32[2,24,4096]{2,0,1:T(2,128)S(1)} %reshape.11), slice={[0:2], [0:19], [0:4096]} | slice | bytes 1245184 | tf_op jit(solution)/shard_map/slice | solution.py:587
  48.5 0.8 %copy.8 = f32[19,8,8,128]{3,2,1,0:T(8,128)} copy(f32[19,8,8,128]{3,2,1,0:T(8,128)S(1)} %get-tuple-element.9) | data formatting | bytes 1245184
Async XLA Ops:
  0.6 1.5 %copy-start.1 = (s32[256]{0:T(256)S(1)}, s32[256]{0:T(256)}, u32[]{:S(2)}) copy-start(s32[256]{0:T(256)} %slots.1) | copy-start | bytes 3076
  0.6 1.5 %copy-start = (f32[19,8,8,128]{3,2,1,0:T(8,128)S(1)}, f32[19,8,8,128]{3,2,1,0:T(8,128)}, u32[]{:S(2)}) copy-start(f32[19,8,8,128]{3,2,1,0:T(8,128)} %coarse.1) | copy-start | bytes 1867780
where the time goes:
time: 49.4 us; the launch traced here: 49.3 us
  Pallas kernels  44.8 us (91%)
  local copies, waits for them, and re-layouts  3.76 us (8%)
  between operations  0.69 us (1%)
    pallas_call x1, Pallas kernels, local(): pl.pallas_call(kernel, out_shape=(jax.ShapeDtypeStruct((1536, 128), jnp.f...  44.8 us
    unnamed x6, local copies, waits for them, and re-layouts  2.34 us

commit v1 on v0

--- a/solution.py
+++ b/solution.py
@@ -288,8 +288,8 @@
 
 
 def kernel(
-    fine, coarse, slots, fine_out, coarse_out,
-    p1, r1, p2, r2, inv_v, inv_s,
+    fine_hbm, coarse_hbm, slots_hbm, fine_out, coarse_out,
+    fine, coarse, slots, si, p1, r1, p2, r2, inv_v, inv_s,
     state, post, mom, tee, face, rows, out1, out2, halo1, halo2,
     layers, low_out, low_in, ghost, edge_r, edge_l, edge_in, ghost_post, ghost_side,
     cmom, face_c, halo_c, rest, rest_out, rest_in, ghost_t, ghost_c, ctee, cpost,
@@ -303,12 +303,17 @@
     for offset in OFFSETS:
         pl.semaphore_signal(barrier, inc=1, device_id=device_of(offset), device_id_type=pl.DeviceIdType.MESH)
 
+    loads = [pltpu.make_async_copy(*pair, si.at[i]) for i, pair in enumerate(((fine_hbm, fine), (slots_hbm, slots), (coarse_hbm, coarse)))]
+    for load in loads:
+        load.start()
+    for load in loads:
+        load.wait()
+
     def pack(t, _):
         for k in range(2):
-            v = fine[k, :, pl.ds(pl.multiple_of(t * 128, 128), 128)]
             for q in range(4):
                 n = min(5, 19 - 5 * q)
-                p1[k, t * 4 + q, 0:n, :] = v[5 * q : 5 * q + n]
+                p1[k, t * 4 + q, 0:n, :] = fine[pl.ds(5 * q * 64 + t * 2 + k, n, stride=64), :]
         return 0
 
     lax.fori_loop(0, 32, pack, 0)
@@ -374,7 +379,7 @@
     for copy in (cm_r, cm_l, cf_r, cf_l):
         copy.start()
 
-    to_ahead.wait()
+    to_ahead.wait_recv()
     for q in range(6):
         for h in range(2):
             v = jnp.where(e == 0, rot(low_in[q, h], -14), low_out[q, h])
@@ -390,21 +395,24 @@
     all1 = r1.at[0:254, 0:5, :]
     pltpu.make_async_copy(all1, all1, s1.at[1]).wait()
 
-    def permute(m, _):
-        for k in range(2):
-            slot = 2 * m + k
-            p2[k, m, 0:5, :] = r1[inv_s[slot // 128, lax.rem(slot, 128)], 0:5, :]
-        return 0
-
-    lax.fori_loop(0, 128, permute, 0, unroll=4)
-    for k in range(2):
-        r2[k, me, 0:5, :] = p2[k, me, 0:5, :]
-    for offset in OFFSETS:
-        x, y = device_of(offset)
-        send(p2.at[:, x * 32 + y, 0:5, :], r2.at[:, me, 0:5, :], s2, (x, y)).start()
-
-    ge_r.wait()
-    ge_l.wait()
+    for start in range(0, 128, 8):
+        group = ([(0, 0, 0, 0)] + OFFSETS)[start : start + 8]
+        targets = [device_of(offset) for offset in group]
+        owners = [x * 32 + y for x, y in targets]
+        found = [[inv_s[m // 64, 2 * lax.rem(m, 64) + k] for k in range(2)] for m in owners]
+        pieces = [[r1[b, 0:5, :] for b in pair] for pair in found]
+        for m, pair in zip(owners, pieces):
+            for k in range(2):
+                p2[k, m, 0:5, :] = pair[k]
+        for m, pair, offset, device in zip(owners, pieces, group, targets):
+            if any(offset):
+                send(p2.at[:, m, 0:5, :], r2.at[:, me, 0:5, :], s2, device).start()
+            else:
+                for k in range(2):
+                    r2[k, me, 0:5, :] = pair[k]
+
+    ge_r.wait_recv()
+    ge_l.wait_recv()
     for q in range(5):
         v = [ghost[q, h] for h in range(2)]
         cx, _, cz = VELOCITIES[Y_PLUS[q]]
@@ -426,7 +434,7 @@
             ghost_side[1, r : r + 1, :] = ghost[5, h, 0:1, :]
             ghost_side[1, 4 + r : 5 + r, :] = ghost[5, h, 7:8, :]
     for copy in (cm_r, cm_l, cf_r, cf_l):
-        copy.wait()
+        copy.wait_recv()
 
     all2 = r2.at[:, 0:127, 0:5, :]
     pltpu.make_async_copy(all2, all2, s2.at[1]).wait()
@@ -463,12 +471,12 @@
     def give(d, tiles):
         for k in range(2):
             for r in range(4):
-                fine_out[pl.ds(((k * 3 + d // 8) * 32 + r) * 8 + d % 8, 8, stride=32), :] = tiles[k * 4 + r]
+                fine_out[pl.ds(d * 64 + r * 2 + k, 8, stride=8), :] = tiles[k * 4 + r]
 
     ghost_pot = [ghost[5, h] for h in range(2)]
     finish = fine_step(state, mom, ghost_pot, ghost_post, ghost_side, halo1, keep, work)
-    f1r.wait()
-    f1l.wait()
+    f1r.wait_recv()
+    f1l.wait_recv()
     finish()
     fine_moments(state, mom)
     fine_faces(state, mom, out2, face)
@@ -477,7 +485,7 @@
     f2r.start()
     f2l.start()
 
-    to_behind.wait()
+    to_behind.wait_recv()
     turned = ghost_t.reshape(6 * 64, 128)
     last = lane() == 127
     for q in range(6):
@@ -493,12 +501,12 @@
     gc_l.start()
 
     finish = fine_step(state, mom, ghost_pot, ghost_post, ghost_side, halo2, give, work)
-    f2r.wait()
-    f2l.wait()
+    f2r.wait_recv()
+    f2l.wait_recv()
     finish()
 
-    gc_r.wait()
-    gc_l.wait()
+    gc_r.wait_recv()
+    gc_l.wait_recv()
 
     def coarse_y(v, step, edge):
         return jnp.where(lane() == (127 if step > 0 else 0), edge, rot(v, -step))
@@ -547,6 +555,8 @@
         return 0
 
     lax.fori_loop(0, 8, stream_body, 0)
+    for copy in (to_ahead, ge_r, ge_l, cm_r, cm_l, cf_r, cf_l, f1r, f1l, f2r, f2l, gc_r, gc_l, to_behind):
+        copy.wait_send()
     pltpu.make_async_copy(all1, all1, s1.at[0]).wait()
     pltpu.make_async_copy(all2, all2, s2.at[0]).wait()
 
@@ -562,12 +572,13 @@
     fine_out, coarse_out = pl.pallas_call(
         kernel,
         out_shape=(
-            jax.ShapeDtypeStruct((1536, 128), jnp.float32),
+            jax.ShapeDtypeStruct((1216, 128), jnp.float32),
             jax.ShapeDtypeStruct((19, 8, 8, 128), jnp.float32),
         ),
-        in_specs=[vmem, vmem, pl.BlockSpec(memory_space=pltpu.SMEM)],
+        in_specs=[pl.BlockSpec(memory_space=pltpu.HBM)] * 3,
         out_specs=(vmem, vmem),
         scratch_shapes=[
+            pltpu.VMEM((1216, 128), jnp.float32), tiles(19, 8), pltpu.SMEM((256,), jnp.int32), sems(3),
             tiles(2, 128), tiles(256), tiles(2, 128), tiles(2, 128),
             pltpu.VMEM((8, 128), jnp.int32), pltpu.SMEM((8, 128), jnp.int32),
             tiles(19, 8), tiles(19, 8), tiles(5, 8), tiles(5, 8), tiles(), tiles(8),
@@ -581,10 +592,10 @@
             sems(2, 2), sems(2, 2), sems(2), sems(2, 2),
         ],
         compiler_params=pltpu.CompilerParams(
-            collective_id=0, has_side_effects=True, vmem_limit_bytes=48 * 2**20
+            collective_id=0, has_side_effects=True, vmem_limit_bytes=53836 * 1024
         ),
-    )(fine_pop, coarse_pop, new_slot)
-    fine_out = fine_out.reshape(2, 3, 32, 8, 128).transpose(0, 1, 3, 2, 4).reshape(2, 24, 4096)[:, :19]
+    )(fine_pop.reshape(2, 19, 32, 128).transpose(1, 2, 0, 3).reshape(1216, 128), coarse_pop, new_slot)
+    fine_out = fine_out.reshape(19, 32, 2, 128).transpose(2, 0, 1, 3).reshape(2, 19, 4096)
     return fine_out, coarse_out
 
 

time: 49.4 us -> 46 us (0.931)
  Pallas kernels: 44.8 us -> 42.8 us
  local copies, waits for them, and re-layouts: 3.76 us -> 2.33 us
    pallas_call x1, Pallas kernels: 44.8 us -> 42.8 us  [local(): pl.pallas_call(kernel, out_shape=(jax.ShapeDtypeStruct((1216, 128), jnp.f...]
    slice x1 -> x0, local copies, waits for them, and re-layouts: 0.87 us -> none  [local(): fine_out.reshape(2, 3, 32, 8, 128).transpose(0, 1, 3, 2, 4)]
    unnamed x6 -> x4, local copies, waits for them, and re-layouts: 2.34 us -> 2.33 us
where the time goes in v1:
time: 46 us; the launch traced here: 45.8 us
  Pallas kernels  42.8 us (93%)
  local copies, waits for them, and re-layouts  2.33 us (5%)
  between operations  0.65 us (1%)
    pallas_call x1, Pallas kernels, local(): pl.pallas_call(kernel, out_shape=(jax.ShapeDtypeStruct((1216, 128), jnp.f...  42.8 us
    unnamed x4, local copies, waits for them, and re-layouts  2.33 us

profile of v1, /device:TPU:0, one launch (start us, length us, event | category | flops | bytes accessed | tf_op | source)
XLA Modules:
  0.0 45.8 jit_solution(13091171159367083304)
XLA Ops:
  0.6 0.0 copy-start
  0.6 0.7 %copy-done = s32[256]{0:T(256)S(1)} copy-done((s32[256]{0:T(256)S(1)}, s32[256]{0:T(256)}, u32[]{:S(2)}) %copy-start) | copy-done | bytes 1048
  1.3 42.8 %shard_map.50 = (f32[1216,128]{1,0:T(8,128)S(1)}, f32[19,8,8,128]{3,2,1,0:T(8,128)S(1)}) custom-call(f32[1216,128]{1,0:T(8,128)} %bitcast.11, f32[19,8,8,128]{3,2,1,0:T(8,128)} %coarse_hbm.1, s32[256]{0:T(256)S(1)} %copy-done), custom_call_target="tpu_custom_call" | custom-call | tf_op jit(solution)/shard_map/pallas_call | solution.py:572
  44.2 0.8 %copy.9 = f32[2,19,4096]{2,0,1:T(2,128)} copy(f32[2,19,4096]{2,0,1:T(2,128)S(1)} %bitcast.10) | data formatting | bytes 1245184
  45.0 0.8 %copy.10 = f32[19,8,8,128]{3,2,1,0:T(8,128)} copy(f32[19,8,8,128]{3,2,1,0:T(8,128)S(1)} %get-tuple-element.9) | data formatting | bytes 1245184
Async XLA Ops:
  0.6 0.7 %copy-start = (s32[256]{0:T(256)S(1)}, s32[256]{0:T(256)}, u32[]{:S(2)}) copy-start(s32[256]{0:T(256)} %slots_hbm.1) | copy-start | bytes 3076

commit v2 on v1

--- a/solution.py
+++ b/solution.py
@@ -292,8 +292,8 @@
     fine, coarse, slots, si, p1, r1, p2, r2, inv_v, inv_s,
     state, post, mom, tee, face, rows, out1, out2, halo1, halo2,
     layers, low_out, low_in, ghost, edge_r, edge_l, edge_in, ghost_post, ghost_side,
-    cmom, face_c, halo_c, rest, rest_out, rest_in, ghost_t, ghost_c, ctee, cpost,
-    s1, s2, s3, sg, se, sc, sm, sh1, sh2, sr, sx,
+    cmom, face_c, halo_c, rest, rest_out, rest_in, ghost_t, ctee, cpost, cgrad, cedge,
+    s1, s2, s3, sg, se, sc, sh1, sh2, sr,
 ):
     g, w = lax.axis_index("grp"), lax.axis_index("wide")
     me = g * 32 + w
@@ -340,6 +340,11 @@
     for q in range(5):
         face_c[0, q] = coarse[X_PLUS[q], 7]
         face_c[1, q] = coarse[X_MINUS[q], 0]
+    for a in range(4):
+        face_c[0, 5 + a] = cmom[a, 9]
+        face_c[1, 5 + a] = cmom[a, 2]
+    face_c[0, 9] = cmom[4, 8]
+    face_c[1, 9] = cmom[4, 3]
 
     flat = coarse.reshape(19 * 64, 128)
     e, c_l, s = lane() & 15, lane() >> 4, sub()
@@ -372,12 +377,10 @@
     for offset in OFFSETS:
         x, y = device_of(offset)
         send(p1.at[:, x * 32 + y, 0:5, :], r1.at[pl.ds(2 * me, 2), 0:5, :], s1, (x, y)).start()
-    cm_r = send(cmom.at[:, 8:10], cmom.at[:, 0:2], sm.at[0], (right, w))
-    cm_l = send(cmom.at[:, 2:4], cmom.at[:, 10:12], sm.at[1], (left, w))
     cf_r = send(face_c.at[0], halo_c.at[0], sc.at[0], (right, w))
     cf_l = send(face_c.at[1], halo_c.at[1], sc.at[1], (left, w))
-    for copy in (cm_r, cm_l, cf_r, cf_l):
-        copy.start()
+    cf_r.start()
+    cf_l.start()
 
     to_ahead.wait_recv()
     for q in range(6):
@@ -433,8 +436,78 @@
             ghost_side[0, 4 + r : 5 + r, :] = edge_in[1, 10 + h : 11 + h, :]
             ghost_side[1, r : r + 1, :] = ghost[5, h, 0:1, :]
             ghost_side[1, 4 + r : 5 + r, :] = ghost[5, h, 7:8, :]
-    for copy in (cm_r, cm_l, cf_r, cf_l):
-        copy.wait_recv()
+    cf_r.wait_recv()
+    cf_l.wait_recv()
+    for side, (near, far) in enumerate(((1, 0), (10, 11))):
+        for a in range(4):
+            cmom[a, near] = halo_c[side, 5 + a]
+        cmom[4, near] = potential(halo_c[side, 5])
+        cmom[4, far] = halo_c[side, 9]
+
+    def coarse_y(v, step):
+        return jnp.where(lane() == (127 if step > 0 else 0), 0.0, rot(v, -step))
+
+    def terms_body(i, _):
+        v = cmom[4, i]
+        t, dy, dz = stencil(v, coarse_y(v, 1), coarse_y(v, -1), turn(v, -1), turn(v, 1))
+        ctee[0, i], ctee[1, i], ctee[2, i] = t, dy, dz
+        return 0
+
+    lax.fori_loop(0, 12, terms_body, 0)
+
+    def coarse_post(i, states):
+        dy, dz = ctee[1, i], ctee[2, i]
+        grad = [
+            ctee[0, i + 1] - ctee[0, i - 1],
+            dy * (1.0 / 18.0) + (ctee[1, i + 1] + ctee[1, i - 1] + turn(dy, 1) + turn(dy, -1)) * (1.0 / 36.0),
+            dz * (1.0 / 18.0) + (ctee[2, i + 1] + ctee[2, i - 1] + coarse_y(dz, 1) + coarse_y(dz, -1)) * (1.0 / 36.0),
+        ]
+        for a in range(3):
+            cgrad[a, i] = grad[a]
+        values = collide([cmom[a, i] for a in range(4)], cmom[4, i], grad, states, COARSE_TAU)
+        for (d, _), v in zip(states, values):
+            cpost[d, i] = v
+
+    def post_body(i, _):
+        coarse_post(i + 2, [(d, coarse[d, i]) for d in range(19)])
+        return 0
+
+    lax.fori_loop(0, 8, post_body, 0)
+    coarse_post(1, [(d, halo_c[0, q]) for q, d in enumerate(X_PLUS)])
+    coarse_post(10, [(d, halo_c[1, q]) for q, d in enumerate(X_MINUS)])
+
+    def stream_body(i, _):
+        for d in range(19):
+            cx, cy, cz = VELOCITIES[d]
+            v = cpost[d, i + 2 - cx]
+            if cz:
+                v = turn(v, cz)
+            if cy:
+                v = rot(v, cy)
+            coarse_out[d, i] = v
+        return 0
+
+    lax.fori_loop(0, 8, stream_body, 0)
+
+    def packed(load, count):
+        v = None
+        for i in count:
+            t = rot(load(i), 2 * i + 1)
+            v = t if v is None else jnp.where(lane() >= 2 * i, t, v)
+        return v
+
+    def edge_body(d, _):
+        cedge[d] = packed(lambda i: coarse[d, i - 2], range(2, 10))
+        return 0
+
+    lax.fori_loop(0, 19, edge_body, 0)
+    for side, (dirs, i) in enumerate(((X_PLUS, 1), (X_MINUS, 10))):
+        for q, d in enumerate(dirs):
+            cedge[d] = jnp.where((lane() >> 1) == i, rot(halo_c[side, q], 2 * i + 1), cedge[d])
+    for a in range(5):
+        cedge[19 + a] = packed(lambda i: cmom[a, i], range(1, 11))
+    for a in range(3):
+        cedge[24 + a] = packed(lambda i: cgrad[a, i], range(1, 11))
 
     all2 = r2.at[:, 0:127, 0:5, :]
     pltpu.make_async_copy(all2, all2, s2.at[1]).wait()
@@ -456,11 +529,18 @@
             v = jnp.where(e < 8, state[d, h] + state[d, 2 + h], state[d, 4 + h] + state[d, 6 + h])
             v = v + rot(v, -1)
             rest[d, h] = 0.125 * (v + rot(v, -16))
+    slot = lane() & 31
     for h in range(2):
+        tile = jnp.zeros((8, 128), jnp.float32)
         for q, v in enumerate(rescaled(rest, e == 14, TO_COARSE, h)):
-            rest_out[q, h] = v
-    to_behind = send(rest_out, rest_in, sr, (g, behind))
-    to_behind.start()
+            tile = jnp.where(slot == 2 * q, rot(v, 2 * q), jnp.where(slot == 2 * q + 1, rot(v, 2 * q - 13), tile))
+        rest_out[h] = tile
+    rests = [
+        send(rest_out, rest_in.at[i], sr.at[i], device)
+        for i, device in enumerate(((g, behind), (right, w), (right, behind), (left, w), (left, behind)))
+    ]
+    for copy in rests:
+        copy.start()
 
     work = (post, tee, face, rows)
 
@@ -485,77 +565,54 @@
     f2r.start()
     f2l.start()
 
-    to_behind.wait_recv()
-    turned = ghost_t.reshape(6 * 64, 128)
-    last = lane() == 127
+    for copy in rests:
+        copy.wait_recv()
+    turned = ghost_t.reshape(192, 128)
+    is_low = (lane() & 1) == 1
+    for b, (low, high) in enumerate(((rest_out, rest_in.at[0]), (rest_in.at[1], rest_in.at[2]), (rest_in.at[3], rest_in.at[4]))):
+        for h in range(2):
+            v = jnp.where(is_low, low[h], high[h])
+            for m in range(4):
+                ghost_t[b, h * 4 + m] = rot(v, -32 * m)
+    starts = [64 + 6, 64 + 7] + list(range(8)) + [128, 129]
+    columns = [turned[pl.ds(r, 8, stride=8), :] for r in starts]
+    entering = []
     for q in range(6):
-        for h in range(2):
-            for m in range(4):
-                low = rot(rest_out[q, h], -(32 * m + 14))
-                ghost_t[q, h * 4 + m] = jnp.where(last, rot(rest_in[q, h], 127 - 32 * m), low)
+        v = rot(columns[0], -2 * q)
+        for i in range(1, 12):
+            v = jnp.where(lane() >= 2 * i, rot(columns[i], 2 * i - 2 * q), v)
+        entering.append(v)
+
+    pg = entering[5]
+    x_up, x_down, z_up, z_down = rot(pg, -2), rot(pg, 2), turn(pg, -1), turn(pg, 1)
+    outward = pg * (1.0 / 18.0) + (x_up + x_down + z_up + z_down) * (1.0 / 36.0)
+    grad = [
+        cedge[24] + (x_up - x_down) * (1.0 / 36.0),
+        cedge[25] + jnp.where(is_low, -outward, outward),
+        cedge[26] + (z_up - z_down) * (1.0 / 36.0),
+    ]
+    again = collide(
+        [cedge[19 + a] for a in range(4)], cedge[23], grad, [(d, cedge[d]) for d in range(19)], COARSE_TAU
+    )
+    for d in range(19):
+        cx, cy, cz = VELOCITIES[d]
+        v = again[d]
+        if cy > 0:
+            v, base, mask = jnp.where(is_low, v, rot(entering[Y_PLUS.index(d)], -1)), 0, lane() < 2
+        elif cy < 0:
+            v, base, mask = jnp.where(is_low, rot(entering[Y_MINUS.index(d)], 1), v), 126, lane() >= 126
+        else:
+            base, mask = 127, (lane() == 0) | (lane() == 127)
+        if cz:
+            v = turn(v, cz)
         for x in range(8):
-            ghost_c[q, x + 2] = turned[pl.ds(q * 64 + x, 8, stride=8), :]
-    gc_r = send(ghost_c.at[:, 8:10], ghost_c.at[:, 0:2], sx.at[0], (right, w))
-    gc_l = send(ghost_c.at[:, 2:4], ghost_c.at[:, 10:12], sx.at[1], (left, w))
-    gc_r.start()
-    gc_l.start()
+            coarse_out[d, x] = jnp.where(mask, rot(v, base - 2 * (x + 2 - cx)), coarse_out[d, x])
 
     finish = fine_step(state, mom, ghost_pot, ghost_post, ghost_side, halo2, give, work)
     f2r.wait_recv()
     f2l.wait_recv()
     finish()
-
-    gc_r.wait_recv()
-    gc_l.wait_recv()
-
-    def coarse_y(v, step, edge):
-        return jnp.where(lane() == (127 if step > 0 else 0), edge, rot(v, -step))
-
-    def terms_body(i, _):
-        v, edge = cmom[4, i], ghost_c[5, i]
-        t, dy, dz = stencil(v, coarse_y(v, 1, edge), coarse_y(v, -1, edge), turn(v, -1), turn(v, 1))
-        ctee[0, i], ctee[1, i], ctee[2, i] = t, dy, dz
-        return 0
-
-    lax.fori_loop(0, 12, terms_body, 0)
-
-    def coarse_grad(i):
-        dy, dz, edge = ctee[1, i], ctee[2, i], ghost_c[5, i]
-        edge = turn(edge, -1) - turn(edge, 1)
-        return [
-            ctee[0, i + 1] - ctee[0, i - 1],
-            dy * (1.0 / 18.0) + (ctee[1, i + 1] + ctee[1, i - 1] + turn(dy, 1) + turn(dy, -1)) * (1.0 / 36.0),
-            dz * (1.0 / 18.0)
-            + (ctee[2, i + 1] + ctee[2, i - 1] + coarse_y(dz, 1, edge) + coarse_y(dz, -1, edge)) * (1.0 / 36.0),
-        ]
-
-    def coarse_post(i, states):
-        values = collide([cmom[a, i] for a in range(4)], cmom[4, i], coarse_grad(i), states, COARSE_TAU)
-        for (d, _), v in zip(states, values):
-            cpost[d, i - 1] = v
-
-    def post_body(i, _):
-        coarse_post(i + 2, [(d, coarse[d, i]) for d in range(19)])
-        return 0
-
-    lax.fori_loop(0, 8, post_body, 0)
-    coarse_post(1, [(d, halo_c[0, q]) for q, d in enumerate(X_PLUS)])
-    coarse_post(10, [(d, halo_c[1, q]) for q, d in enumerate(X_MINUS)])
-
-    def stream_body(i, _):
-        for d in range(19):
-            cx, cy, cz = VELOCITIES[d]
-            v = cpost[d, i + 1 - cx]
-            if cz:
-                v = turn(v, cz)
-            if cy:
-                edge = ghost_c[(Y_PLUS if cy > 0 else Y_MINUS).index(d), i + 2 - cx]
-                v = coarse_y(v, -cy, turn(edge, cz) if cz else edge)
-            coarse_out[d, i] = v
-        return 0
-
-    lax.fori_loop(0, 8, stream_body, 0)
-    for copy in (to_ahead, ge_r, ge_l, cm_r, cm_l, cf_r, cf_l, f1r, f1l, f2r, f2l, gc_r, gc_l, to_behind):
+    for copy in (to_ahead, ge_r, ge_l, cf_r, cf_l, f1r, f1l, f2r, f2l, *rests):
         copy.wait_send()
     pltpu.make_async_copy(all1, all1, s1.at[0]).wait()
     pltpu.make_async_copy(all2, all2, s2.at[0]).wait()
@@ -586,10 +643,10 @@
             tiles(19, 2), tiles(6, 2), tiles(6, 2), tiles(6, 2),
             pltpu.VMEM((12, 128), jnp.float32), pltpu.VMEM((12, 128), jnp.float32),
             pltpu.VMEM((2, 12, 128), jnp.float32), tiles(5, 4), tiles(2),
-            tiles(5, 12), tiles(2, 5), tiles(2, 5), tiles(19, 2), tiles(6, 2), tiles(6, 2),
-            tiles(6, 8), tiles(6, 12), tiles(3, 12), tiles(19, 10),
-            sems(2), sems(2), pltpu.SemaphoreType.DMA, sems(2), sems(2, 2), sems(2, 2), sems(2, 2),
-            sems(2, 2), sems(2, 2), sems(2), sems(2, 2),
+            tiles(5, 12), tiles(2, 10), tiles(2, 10), tiles(19, 2), tiles(2), tiles(5, 2),
+            tiles(3, 8), tiles(3, 12), tiles(19, 12), tiles(3, 12), tiles(27),
+            sems(2), sems(2), pltpu.SemaphoreType.DMA, sems(2), sems(2, 2), sems(2, 2),
+            sems(2, 2), sems(2, 2), sems(5, 2),
         ],
         compiler_params=pltpu.CompilerParams(
             collective_id=0, has_side_effects=True, vmem_limit_bytes=53836 * 1024

time: 46 us -> 43.6 us (0.948)
  Pallas kernels: 42.8 us -> 40.5 us
    pallas_call x1, Pallas kernels: 42.8 us -> 40.5 us  [local(): pl.pallas_call(kernel, out_shape=(jax.ShapeDtypeStruct((1216, 128), jnp.f...]
where the time goes in v2:
time: 43.6 us; the launch traced here: 43.5 us
  Pallas kernels  40.5 us (93%)
  local copies, waits for them, and re-layouts  2.33 us (5%)
  between operations  0.65 us (1%)
    pallas_call x1, Pallas kernels, local(): pl.pallas_call(kernel, out_shape=(jax.ShapeDtypeStruct((1216, 128), jnp.f...  40.5 us
    unnamed x4, local copies, waits for them, and re-layouts  2.33 us

profile of v2, /device:TPU:0, one launch (start us, length us, event | category | flops | bytes accessed | tf_op | source)
XLA Modules:
  0.0 43.5 jit_solution(13256694895079423874)
XLA Ops:
  0.6 0.0 copy-start
  0.6 0.7 %copy-done = s32[256]{0:T(256)S(1)} copy-done((s32[256]{0:T(256)S(1)}, s32[256]{0:T(256)}, u32[]{:S(2)}) %copy-start) | copy-done | bytes 1048
  1.3 40.5 %shard_map.50 = (f32[1216,128]{1,0:T(8,128)S(1)}, f32[19,8,8,128]{3,2,1,0:T(8,128)S(1)}) custom-call(f32[1216,128]{1,0:T(8,128)} %bitcast.11, f32[19,8,8,128]{3,2,1,0:T(8,128)} %coarse_hbm.1, s32[256]{0:T(256)S(1)} %copy-done), custom_call_target="tpu_custom_call" | custom-call | tf_op jit(solution)/shard_map/pallas_call | solution.py:629
  41.8 0.8 %copy.9 = f32[2,19,4096]{2,0,1:T(2,128)} copy(f32[2,19,4096]{2,0,1:T(2,128)S(1)} %bitcast.10) | data formatting | bytes 1245184
  42.6 0.8 %copy.10 = f32[19,8,8,128]{3,2,1,0:T(8,128)} copy(f32[19,8,8,128]{3,2,1,0:T(8,128)S(1)} %get-tuple-element.9) | data formatting | bytes 1245184
Async XLA Ops:
  0.6 0.7 %copy-start = (s32[256]{0:T(256)S(1)}, s32[256]{0:T(256)}, u32[]{:S(2)}) copy-start(s32[256]{0:T(256)} %slots_hbm.1) | copy-start | bytes 3076

commit v3 on v2

--- a/solution.py
+++ b/solution.py
@@ -39,6 +39,7 @@
 Y_PLUS = (3, 7, 10, 15, 17)
 Y_MINUS = tuple(INDEX[(c[0], -c[1], c[2])] for c in (VELOCITIES[i] for i in Y_PLUS))
 
+PARTS = ((0, 1), (1, 2), (2, 5))
 OFFSETS = sorted(
     ((a, b, c, d) for a in range(4) for b in range(4) for c in range(4) for d in range(2) if a + b + c + d),
     key=lambda o: (-sum(min(v, 4 - v) for v in o[:3]), (o[0] * 7 + o[1] * 5 + o[2] * 3 + o[3]) % 11),
@@ -289,7 +290,7 @@
 
 def kernel(
     fine_hbm, coarse_hbm, slots_hbm, fine_out, coarse_out,
-    fine, coarse, slots, si, p1, r1, p2, r2, inv_v, inv_s,
+    fine, coarse, slots, si, p1, r1_0, r1_1, r1_2, p2, r2, inv_v, inv_s,
     state, post, mom, tee, face, rows, out1, out2, halo1, halo2,
     layers, low_out, low_in, ghost, edge_r, edge_l, edge_in, ghost_post, ghost_side,
     cmom, face_c, halo_c, rest, rest_out, rest_in, ghost_t, ctee, cpost, cgrad, cedge,
@@ -300,6 +301,7 @@
     right, left = lax.rem(g + 1, 4), lax.rem(g + 3, 4)
     ahead, behind = lax.rem(w + 1, 32), lax.rem(w + 31, 32)
     barrier = pltpu.get_barrier_semaphore()
+    r1 = (r1_0, r1_1, r1_2)
     for offset in OFFSETS:
         pl.semaphore_signal(barrier, inc=1, device_id=device_of(offset), device_id_type=pl.DeviceIdType.MESH)
 
@@ -327,7 +329,8 @@
     fetch = pltpu.make_async_copy(inv_v, inv_s, s3)
     fetch.start()
     for k in range(2):
-        r1[2 * me + k, 0:5, :] = p1[k, me, 0:5, :]
+        for part, (lo, hi) in enumerate(PARTS):
+            r1[part][2 * me + k, lo:hi, :] = p1[k, me, lo:hi, :]
 
     def coarse_body(i, _):
         values = moments([coarse[d, i] for d in range(19)])
@@ -374,9 +377,10 @@
     pl.semaphore_wait(barrier, len(OFFSETS))
     to_ahead = send(low_out, low_in, sg, (g, ahead))
     to_ahead.start()
-    for offset in OFFSETS:
-        x, y = device_of(offset)
-        send(p1.at[:, x * 32 + y, 0:5, :], r1.at[pl.ds(2 * me, 2), 0:5, :], s1, (x, y)).start()
+    for part, (lo, hi) in enumerate(PARTS):
+        for offset in OFFSETS:
+            x, y = device_of(offset)
+            send(p1.at[:, x * 32 + y, lo:hi, :], r1[part].at[pl.ds(2 * me, 2), lo:hi, :], s1.at[part], (x, y)).start()
     cf_r = send(face_c.at[0], halo_c.at[0], sc.at[0], (right, w))
     cf_l = send(face_c.at[1], halo_c.at[1], sc.at[1], (left, w))
     cf_r.start()
@@ -395,24 +399,26 @@
     ge_l.start()
 
     fetch.wait()
-    all1 = r1.at[0:254, 0:5, :]
-    pltpu.make_async_copy(all1, all1, s1.at[1]).wait()
-
-    for start in range(0, 128, 8):
-        group = ([(0, 0, 0, 0)] + OFFSETS)[start : start + 8]
-        targets = [device_of(offset) for offset in group]
-        owners = [x * 32 + y for x, y in targets]
-        found = [[inv_s[m // 64, 2 * lax.rem(m, 64) + k] for k in range(2)] for m in owners]
-        pieces = [[r1[b, 0:5, :] for b in pair] for pair in found]
-        for m, pair in zip(owners, pieces):
-            for k in range(2):
-                p2[k, m, 0:5, :] = pair[k]
-        for m, pair, offset, device in zip(owners, pieces, group, targets):
-            if any(offset):
-                send(p2.at[:, m, 0:5, :], r2.at[:, me, 0:5, :], s2, device).start()
-            else:
+
+    everyone = [(0, 0, 0, 0)] + OFFSETS
+    for part, (lo, hi) in enumerate(PARTS):
+        arrived = r1[part].at[0:254, lo:hi, :]
+        pltpu.make_async_copy(arrived, arrived, s1.at[part, 1]).wait()
+        for start in range(0, 128, 8):
+            group = everyone[start : start + 8]
+            targets = [device_of(offset) for offset in group]
+            owners = [x * 32 + y for x, y in targets]
+            found = [[inv_s[m // 64, 2 * lax.rem(m, 64) + k] for k in range(2)] for m in owners]
+            pieces = [[r1[part][b, lo:hi, :] for b in pair] for pair in found]
+            for m, pair in zip(owners, pieces):
                 for k in range(2):
-                    r2[k, me, 0:5, :] = pair[k]
+                    p2[k, m, lo:hi, :] = pair[k]
+            for m, pair, offset, device in zip(owners, pieces, group, targets):
+                if any(offset):
+                    send(p2.at[:, m, lo:hi, :], r2.at[:, me, lo:hi, :], s2.at[part], device).start()
+                else:
+                    for k in range(2):
+                        r2[k, me, lo:hi, :] = pair[k]
 
     ge_r.wait_recv()
     ge_l.wait_recv()
@@ -509,8 +515,9 @@
     for a in range(3):
         cedge[24 + a] = packed(lambda i: cgrad[a, i], range(1, 11))
 
-    all2 = r2.at[:, 0:127, 0:5, :]
-    pltpu.make_async_copy(all2, all2, s2.at[1]).wait()
+    for part, (lo, hi) in enumerate(PARTS):
+        arrived = r2.at[:, 0:127, lo:hi, :]
+        pltpu.make_async_copy(arrived, arrived, s2.at[part, 1]).wait()
     got = r2.reshape(2048, 128)
     for d in range(19):
         for k in range(2):
@@ -614,8 +621,9 @@
     finish()
     for copy in (to_ahead, ge_r, ge_l, cf_r, cf_l, f1r, f1l, f2r, f2l, *rests):
         copy.wait_send()
-    pltpu.make_async_copy(all1, all1, s1.at[0]).wait()
-    pltpu.make_async_copy(all2, all2, s2.at[0]).wait()
+    for part, (lo, hi) in enumerate(PARTS):
+        for left_here, sems in ((r1[part].at[0:254, lo:hi, :], s1), (r2.at[:, 0:127, lo:hi, :], s2)):
+            pltpu.make_async_copy(left_here, left_here, sems.at[part, 0]).wait()
 
 
 def local(fine_pop, coarse_pop, new_slot):
@@ -636,7 +644,7 @@
         out_specs=(vmem, vmem),
         scratch_shapes=[
             pltpu.VMEM((1216, 128), jnp.float32), tiles(19, 8), pltpu.SMEM((256,), jnp.int32), sems(3),
-            tiles(2, 128), tiles(256), tiles(2, 128), tiles(2, 128),
+            tiles(2, 128), tiles(256), tiles(256), tiles(256), tiles(2, 128), tiles(2, 128),
             pltpu.VMEM((8, 128), jnp.int32), pltpu.SMEM((8, 128), jnp.int32),
             tiles(19, 8), tiles(19, 8), tiles(5, 8), tiles(5, 8), tiles(), tiles(8),
             tiles(10), tiles(10), tiles(10), tiles(10),
@@ -645,7 +653,7 @@
             pltpu.VMEM((2, 12, 128), jnp.float32), tiles(5, 4), tiles(2),
             tiles(5, 12), tiles(2, 10), tiles(2, 10), tiles(19, 2), tiles(2), tiles(5, 2),
             tiles(3, 8), tiles(3, 12), tiles(19, 12), tiles(3, 12), tiles(27),
-            sems(2), sems(2), pltpu.SemaphoreType.DMA, sems(2), sems(2, 2), sems(2, 2),
+            sems(len(PARTS), 2), sems(len(PARTS), 2), pltpu.SemaphoreType.DMA, sems(2), sems(2, 2), sems(2, 2),
             sems(2, 2), sems(2, 2), sems(5, 2),
         ],
         compiler_params=pltpu.CompilerParams(

time: 43.6 us -> 41.3 us (0.947)
  Pallas kernels: 40.5 us -> 38.2 us
    pallas_call x1, Pallas kernels: 40.5 us -> 38.2 us  [local(): pl.pallas_call(kernel, out_shape=(jax.ShapeDtypeStruct((1216, 128), jnp.f...]
where the time goes in v3:
time: 41.3 us; the launch traced here: 41.2 us
  Pallas kernels  38.2 us (92%)
  local copies, waits for them, and re-layouts  2.33 us (6%)
  between operations  0.65 us (2%)
    pallas_call x1, Pallas kernels, local(): pl.pallas_call(kernel, out_shape=(jax.ShapeDtypeStruct((1216, 128), jnp.f...  38.2 us
    unnamed x4, local copies, waits for them, and re-layouts  2.33 us

profile of v3, /device:TPU:0, one launch (start us, length us, event | category | flops | bytes accessed | tf_op | source)
XLA Modules:
  0.0 41.2 jit_solution(16697044095710009706)
XLA Ops:
  0.6 0.0 copy-start
  0.6 0.7 %copy-done = s32[256]{0:T(256)S(1)} copy-done((s32[256]{0:T(256)S(1)}, s32[256]{0:T(256)}, u32[]{:S(2)}) %copy-start) | copy-done | bytes 1048
  1.3 38.2 %shard_map.50 = (f32[1216,128]{1,0:T(8,128)S(1)}, f32[19,8,8,128]{3,2,1,0:T(8,128)S(1)}) custom-call(f32[1216,128]{1,0:T(8,128)} %bitcast.11, f32[19,8,8,128]{3,2,1,0:T(8,128)} %coarse_hbm.1, s32[256]{0:T(256)S(1)} %copy-done), custom_call_target="tpu_custom_call" | custom-call | tf_op jit(solution)/shard_map/pallas_call | solution.py:637
  39.5 0.8 %copy.9 = f32[2,19,4096]{2,0,1:T(2,128)} copy(f32[2,19,4096]{2,0,1:T(2,128)S(1)} %bitcast.10) | data formatting | bytes 1245184
  40.4 0.8 %copy.10 = f32[19,8,8,128]{3,2,1,0:T(8,128)} copy(f32[19,8,8,128]{3,2,1,0:T(8,128)S(1)} %get-tuple-element.9) | data formatting | bytes 1245184
Async XLA Ops:
  0.6 0.7 %copy-start = (s32[256]{0:T(256)S(1)}, s32[256]{0:T(256)}, u32[]{:S(2)}) copy-start(s32[256]{0:T(256)} %slots_hbm.1) | copy-start | bytes 3076

commit v4 on v3

--- a/solution.py
+++ b/solution.py
@@ -302,12 +302,12 @@
     ahead, behind = lax.rem(w + 1, 32), lax.rem(w + 31, 32)
     barrier = pltpu.get_barrier_semaphore()
     r1 = (r1_0, r1_1, r1_2)
-    for offset in OFFSETS:
-        pl.semaphore_signal(barrier, inc=1, device_id=device_of(offset), device_id_type=pl.DeviceIdType.MESH)
-
     loads = [pltpu.make_async_copy(*pair, si.at[i]) for i, pair in enumerate(((fine_hbm, fine), (slots_hbm, slots), (coarse_hbm, coarse)))]
     for load in loads:
         load.start()
+    for offset in OFFSETS:
+        pl.semaphore_signal(barrier, inc=1, device_id=device_of(offset), device_id_type=pl.DeviceIdType.MESH)
+
     for load in loads:
         load.wait()
 

time: 41.3 us -> 40.5 us (0.981)
  Pallas kernels: 38.2 us -> 37.4 us
    pallas_call x1, Pallas kernels: 38.2 us -> 37.4 us  [local(): pl.pallas_call(kernel, out_shape=(jax.ShapeDtypeStruct((1216, 128), jnp.f...]
where the time goes in v4:
time: 40.5 us; the launch traced here: 40.4 us
  Pallas kernels  37.4 us (92%)
  local copies, waits for them, and re-layouts  2.33 us (6%)
  between operations  0.65 us (2%)
    pallas_call x1, Pallas kernels, local(): pl.pallas_call(kernel, out_shape=(jax.ShapeDtypeStruct((1216, 128), jnp.f...  37.4 us
    unnamed x4, local copies, waits for them, and re-layouts  2.33 us

profile of v4, /device:TPU:0, one launch (start us, length us, event | category | flops | bytes accessed | tf_op | source)
XLA Modules:
  0.0 40.4 jit_solution(6206338602393796927)
XLA Ops:
  0.6 0.0 copy-start
  0.6 0.7 %copy-done = s32[256]{0:T(256)S(1)} copy-done((s32[256]{0:T(256)S(1)}, s32[256]{0:T(256)}, u32[]{:S(2)}) %copy-start) | copy-done | bytes 1048
  1.3 37.4 %shard_map.50 = (f32[1216,128]{1,0:T(8,128)S(1)}, f32[19,8,8,128]{3,2,1,0:T(8,128)S(1)}) custom-call(f32[1216,128]{1,0:T(8,128)} %bitcast.11, f32[19,8,8,128]{3,2,1,0:T(8,128)} %coarse_hbm.1, s32[256]{0:T(256)S(1)} %copy-done), custom_call_target="tpu_custom_call" | custom-call | tf_op jit(solution)/shard_map/pallas_call | solution.py:637
  38.7 0.8 %copy.9 = f32[2,19,4096]{2,0,1:T(2,128)} copy(f32[2,19,4096]{2,0,1:T(2,128)S(1)} %bitcast.10) | data formatting | bytes 1245184
  39.5 0.8 %copy.10 = f32[19,8,8,128]{3,2,1,0:T(8,128)} copy(f32[19,8,8,128]{3,2,1,0:T(8,128)S(1)} %get-tuple-element.9) | data formatting | bytes 1245184
Async XLA Ops:
  0.6 0.7 %copy-start = (s32[256]{0:T(256)S(1)}, s32[256]{0:T(256)}, u32[]{:S(2)}) copy-start(s32[256]{0:T(256)} %slots_hbm.1) | copy-start | bytes 3076
